TPU v7x, 1024 devices: a whole 4x4x32 slice. The times are simulated.
1024 devices in a mesh: space: 128 (over x, y, z_hi, core), param: 8 (over z_lo).
Axes of the slice: x: 4, y: 4, z: 32 (z_hi: 4, z_lo: 8; z = z_hi * 8 + z_lo), core: 2. Of those that a mesh axis runs over, the one named last changes fastest.
Arguments:
- grain_param: int32 [128, 8, 8, 128], P('space'), may hold values from 0 to 127, as said below
- perturbation: float32 [128, 128, 8, 8, 128], P('param', 'space'), may hold values from -0.2 to 0.2
- mobility: float32 [128, 8, 8, 128], P('space'), may hold values from 0.25 to 2.5
Outputs:
- fields: float32 [128, 128, 8, 8, 128], P('param', 'space')
Inputs may be any that keep to these rules, and one draw needn't show every extreme that they name: `grain_param`: in the grid, constant on aligned blocks of 2 x 2 x 4 cells; every one of the 128 order parameters is the value of some block.
All inputs are finite; a program needn't handle non-finite values.
Results may differ from a plain program's by a relative error of at most 0.0003.
Values sent between devices are 32-bit elements; how exact they have to be, the bound alone decides.
A program may use at most 32 MiB of HBM per device.

v0:
```python
import jax
import jax.numpy as jnp
from jax import lax
from jax.sharding import PartitionSpec as P

OUTER = 2
SUB = 2


time_step = 0.05
cross_weight = 1.5


def with_halo(cells, sides, width):
    for axis, dim in sides:
        count = lax.axis_size(axis)
        ends = count - 1
        head = lax.slice_in_dim(cells, 0, width, axis=dim)
        tail = lax.slice_in_dim(cells, cells.shape[dim] - width, cells.shape[dim], axis=dim)
        cells = jnp.concatenate(
            [
                lax.ppermute(tail, axis, [(i, (i + 1) % count) for i in range(ends)]),
                cells,
                lax.ppermute(head, axis, [((i + 1) % count, i) for i in range(ends)]),
            ],
            axis=dim,
        )
    return cells


def advance(padded, totals, x_start, y_start, extent_x, extent_y):
    values = padded[:-1]
    moving = padded[-1]
    span_x = values.shape[1]
    span_y = values.shape[2]
    depth_z = values.shape[3]
    place_x = x_start + jnp.arange(span_x, dtype=jnp.int32)
    place_y = y_start + jnp.arange(span_y, dtype=jnp.int32)
    open_x = ((place_x[:-1] >= 0) & (place_x[1:] <= extent_x - 1)).astype(values.dtype)
    open_y = ((place_y[:-1] >= 0) & (place_y[1:] <= extent_y - 1)).astype(values.dtype)
    face_x = 0.5 * (moving[:-1] + moving[1:]) * open_x[:, None, None]
    flow_x = face_x[None] * (values[:, 1:] - values[:, :-1])
    summed = (flow_x[:, 1:] - flow_x[:, :-1])[:, :, 1:-1]
    middle = values[:, 1:-1]
    mobility_rows = moving[1:-1]
    face_y = 0.5 * (mobility_rows[:, :-1] + mobility_rows[:, 1:]) * open_y[None, :, None]
    flow_y = face_y[None] * (middle[:, :, 1:] - middle[:, :, :-1])
    summed = summed + flow_y[:, :, 1:] - flow_y[:, :, :-1]
    centre = middle[:, :, 1:-1]
    mobility_centre = mobility_rows[:, 1:-1]
    open_z = (jnp.arange(depth_z) < depth_z - 1).astype(values.dtype)
    face_z = 0.5 * (mobility_centre + jnp.roll(mobility_centre, -1, 2)) * open_z
    flow_z = face_z[None] * (jnp.roll(centre, -1, 3) - centre)
    summed = summed + flow_z - jnp.roll(flow_z, 1, 3)
    reaction = (
        centre * centre * centre
        - centre
        + 2.0 * cross_weight * centre * (totals[None] - centre * centre)
    )
    updated = centre + time_step * (summed - mobility_centre[None] * reaction)
    return jnp.concatenate([updated, mobility_centre[None]], axis=0)


def extend(block, margin_width):
    lower_rows = block[:, :, :margin_width]
    upper_rows = block[:, :, -margin_width:]
    rim_rows = jnp.concatenate([lower_rows, upper_rows], axis=2)
    haloed = with_halo(rim_rows, (("space", 2),), margin_width)
    widened = jnp.concatenate(
        [haloed[:, :, :margin_width], block, haloed[:, :, 3 * margin_width :]], axis=2
    )
    return jnp.pad(widened, ((0, 0), (margin_width, margin_width), (0, 0), (0, 0)))


def square_total(values):
    return lax.psum(jnp.sum(values * values, axis=0), "param")


def local(grain_param, perturbation, mobility):
    local_count = perturbation.shape[0]
    tile_rows = grain_param.shape[1]
    tile_cols = grain_param.shape[2]
    tile_count = lax.axis_size("space")
    tile_index = lax.axis_index("space")
    extent_y = tile_count * tile_cols
    corner_x = 0
    corner_y = tile_index * tile_cols
    labels = lax.axis_index("param") * local_count + jnp.arange(local_count, dtype=jnp.int32)
    fields = (
        jnp.where(grain_param[0][None] == labels[:, None, None, None], 1.0, 0.0).astype(jnp.float32)
        + perturbation[:, 0]
    )
    mobility_cells = mobility[0][None]
    margin_width = 1
    for _ in range(OUTER):
        totals = square_total(fields)
        for substep in range(SUB):
            block_step = substep % margin_width
            padded = extend(jnp.concatenate([fields, mobility_cells], axis=0), margin_width)
            current = margin_width - block_step
            padded = advance(
                padded, totals, corner_x - current, corner_y - current, tile_rows, extent_y
            )
            fields = padded[:-1]
    return fields[:, None]


def solution(mesh):
    in_specs = (
        P("space", None, None, None),
        P("param", "space", None, None, None),
        P("space", None, None, None),
    )
    out_specs = P("param", "space", None, None, None)
    return jax.shard_map(local, mesh=mesh, in_specs=in_specs, out_specs=out_specs, check_vma=False)
```

profile of v0, /device:TPU:6, one launch (start us, length us, event | category | flops | bytes accessed | tf_op | source)
XLA Modules:
  0.0 196.0 jit_solution(16489918974074833157)
XLA Ops:
  0.0 1.2 multiply_reduce_fusion.1
  1.3 1.9 collective-permute-start
  3.3 25.2 %collective-permute-start.1 = (f32[17,8,1,128]{3,2,1,0:T(1,128)S(1)}, f32[17,8,1,128]{3,2,1,0:T(1,128)S(1)}, u32[]{:S(2)}, u32[]{:S(2)}) collective-permute-start(f32[17,8,1,128]{3,2,1,0:T(1,128)S(1)} %get-tuple-element.24), channel_id=1, source_target_pairs={{8,0},{16,8},{24,16},{32,24},{40,32},{48,40},{56,48},{64,56},{72,6... | collective-permute-start | bytes 208904 | tf_op jit(solution)/shard_map/ppermute | solution.py:24
  28.8 52.4 %psum.14 = f32[8,8,128]{2,1,0:T(8,128)S(1)} all-reduce(f32[8,8,128]{2,1,0:T(8,128)S(1)} %get-tuple-element.7), channel_id=1, replica_groups=mesh['space'=128,'param'=8] {'param'}, use_global_device_ids=true, to_apply=%region_1.2 | all-reduce | flops 8192 | bytes 65536 | tf_op jit(solution)/shard_map/psum | solution.py:76
  81.9 0.2 fusion.65
  82.5 0.2 fusion.18
  82.7 0.5 fusion.37
  83.3 1.9 collective-permute-start.2
  85.3 15.4 %collective-permute-start.3 = (f32[17,8,1,128]{3,2,1,0:T(1,128)S(1)}, f32[17,8,1,128]{3,2,1,0:T(1,128)S(1)}, u32[]{:S(2)}, u32[]{:S(2)}) collective-permute-start(f32[17,8,1,128]{3,2,1,0:T(1,128)S(1)} %get-tuple-element.22), channel_id=1, source_target_pairs={{8,0},{16,8},{24,16},{32,24},{40,32},{48,40},{56,48},{64,56},{72,6... | collective-permute-start | bytes 208904 | tf_op jit(solution)/shard_map/ppermute | solution.py:24
  101.0 2.1 %collective-permute-done.3 = f32[17,8,1,128]{3,2,1,0:T(1,128)S(1)} collective-permute-done((f32[17,8,1,128]{3,2,1,0:T(1,128)S(1)}, f32[17,8,1,128]{3,2,1,0:T(1,128)S(1)}, u32[]{:S(2)}, u32[]{:S(2)}) %collective-permute-start.3) | collective-permute-done | bytes 69664 | tf_op jit(solution)/shard_map/ppermute | solution.py:24
  103.1 0.2 fusion.11
  103.8 0.2 fusion.66
  104.6 0.5 multiply_reduce_fusion
  105.2 7.0 %collective-permute-start.4 = (f32[17,8,1,128]{3,2,1,0:T(1,128)S(1)}, f32[17,8,1,128]{3,2,1,0:T(1,128)S(1)}, u32[]{:S(2)}, u32[]{:S(2)}) collective-permute-start(f32[17,8,1,128]{3,2,1,0:T(1,128)S(1)} %get-tuple-element.19), channel_id=1, source_target_pairs={{0,8},{8,16},{16,24},{24,32},{32,40},{40,48},{48,56},{56,64},{64,7... | collective-permute-start | bytes 208904 | tf_op jit(solution)/shard_map/ppermute | solution.py:22
  112.2 10.6 %collective-permute-start.5 = (f32[17,8,1,128]{3,2,1,0:T(1,128)S(1)}, f32[17,8,1,128]{3,2,1,0:T(1,128)S(1)}, u32[]{:S(2)}, u32[]{:S(2)}) collective-permute-start(f32[17,8,1,128]{3,2,1,0:T(1,128)S(1)} %get-tuple-element.20), channel_id=1, source_target_pairs={{8,0},{16,8},{24,16},{32,24},{40,32},{48,40},{56,48},{64,56},{72,6... | collective-permute-start | bytes 208904 | tf_op jit(solution)/shard_map/ppermute | solution.py:24
  123.0 48.8 %psum.15 = f32[8,8,128]{2,1,0:T(8,128)S(1)} all-reduce(f32[8,8,128]{2,1,0:T(8,128)S(1)} %get-tuple-element.5), channel_id=1, replica_groups=mesh['space'=128,'param'=8] {'param'}, use_global_device_ids=true, to_apply=%region_3.4 | all-reduce | flops 8192 | bytes 65536 | tf_op jit(solution)/shard_map/psum | solution.py:76
  172.6 0.2 fusion.67
  173.2 0.2 fusion.24
  173.4 0.5 fusion.43
  174.0 1.9 collective-permute-start.6
  175.9 15.4 %collective-permute-start.7 = (f32[17,8,1,128]{3,2,1,0:T(1,128)S(1)}, f32[17,8,1,128]{3,2,1,0:T(1,128)S(1)}, u32[]{:S(2)}, u32[]{:S(2)}) collective-permute-start(f32[17,8,1,128]{3,2,1,0:T(1,128)S(1)} %get-tuple-element.18), channel_id=1, source_target_pairs={{8,0},{16,8},{24,16},{32,24},{40,32},{48,40},{56,48},{64,56},{72,6... | collective-permute-start | bytes 208904 | tf_op jit(solution)/shard_map/ppermute | solution.py:24
  191.5 1.7 collective-permute-done.7
  193.2 0.2 fusion.15
  194.7 1.3 fusion.56
  (63 shorter events, 5.9 us)
Async XLA Ops:
  0.0 1.2 copy-start
  1.3 79.9 %collective-permute-start = (f32[17,8,1,128]{3,2,1,0:T(1,128)S(1)}, f32[17,8,1,128]{3,2,1,0:T(1,128)S(1)}, u32[]{:S(2)}, u32[]{:S(2)}) collective-permute-start(f32[17,8,1,128]{3,2,1,0:T(1,128)S(1)} %get-tuple-element.23), channel_id=1, source_target_pairs={{0,8},{8,16},{16,24},{24,32},{32,40},{40,48},{48,56},{56,64},{64,7... | collective-permute-start | bytes 208904 | tf_op jit(solution)/shard_map/ppermute | solution.py:22
  3.3 78.0 %collective-permute-start.1 = (f32[17,8,1,128]{3,2,1,0:T(1,128)S(1)}, f32[17,8,1,128]{3,2,1,0:T(1,128)S(1)}, u32[]{:S(2)}, u32[]{:S(2)}) collective-permute-start(f32[17,8,1,128]{3,2,1,0:T(1,128)S(1)} %get-tuple-element.24), channel_id=1, source_target_pairs={{8,0},{16,8},{24,16},{32,24},{40,32},{48,40},{56,48},{64,56},{72,6... | collective-permute-start | bytes 208904 | tf_op jit(solution)/shard_map/ppermute | solution.py:24
  83.3 17.7 %collective-permute-start.2 = (f32[17,8,1,128]{3,2,1,0:T(1,128)S(1)}, f32[17,8,1,128]{3,2,1,0:T(1,128)S(1)}, u32[]{:S(2)}, u32[]{:S(2)}) collective-permute-start(f32[17,8,1,128]{3,2,1,0:T(1,128)S(1)} %get-tuple-element.21), channel_id=1, source_target_pairs={{0,8},{8,16},{16,24},{24,32},{32,40},{40,48},{48,56},{56,64},{64,7... | collective-permute-start | bytes 208904 | tf_op jit(solution)/shard_map/ppermute | solution.py:22
  85.3 17.9 %collective-permute-start.3 = (f32[17,8,1,128]{3,2,1,0:T(1,128)S(1)}, f32[17,8,1,128]{3,2,1,0:T(1,128)S(1)}, u32[]{:S(2)}, u32[]{:S(2)}) collective-permute-start(f32[17,8,1,128]{3,2,1,0:T(1,128)S(1)} %get-tuple-element.22), channel_id=1, source_target_pairs={{8,0},{16,8},{24,16},{32,24},{40,32},{48,40},{56,48},{64,56},{72,6... | collective-permute-start | bytes 208904 | tf_op jit(solution)/shard_map/ppermute | solution.py:24
  105.2 66.6 %collective-permute-start.4 = (f32[17,8,1,128]{3,2,1,0:T(1,128)S(1)}, f32[17,8,1,128]{3,2,1,0:T(1,128)S(1)}, u32[]{:S(2)}, u32[]{:S(2)}) collective-permute-start(f32[17,8,1,128]{3,2,1,0:T(1,128)S(1)} %get-tuple-element.19), channel_id=1, source_target_pairs={{0,8},{8,16},{16,24},{24,32},{32,40},{40,48},{48,56},{56,64},{64,7... | collective-permute-start | bytes 208904 | tf_op jit(solution)/shard_map/ppermute | solution.py:22
  112.2 59.6 %collective-permute-start.5 = (f32[17,8,1,128]{3,2,1,0:T(1,128)S(1)}, f32[17,8,1,128]{3,2,1,0:T(1,128)S(1)}, u32[]{:S(2)}, u32[]{:S(2)}) collective-permute-start(f32[17,8,1,128]{3,2,1,0:T(1,128)S(1)} %get-tuple-element.20), channel_id=1, source_target_pairs={{8,0},{16,8},{24,16},{32,24},{40,32},{48,40},{56,48},{64,56},{72,6... | collective-permute-start | bytes 208904 | tf_op jit(solution)/shard_map/ppermute | solution.py:24
  174.0 17.5 %collective-permute-start.6 = (f32[17,8,1,128]{3,2,1,0:T(1,128)S(1)}, f32[17,8,1,128]{3,2,1,0:T(1,128)S(1)}, u32[]{:S(2)}, u32[]{:S(2)}) collective-permute-start(f32[17,8,1,128]{3,2,1,0:T(1,128)S(1)} %get-tuple-element.17), channel_id=1, source_target_pairs={{0,8},{8,16},{16,24},{24,32},{32,40},{40,48},{48,56},{56,64},{64,7... | collective-permute-start | bytes 208904 | tf_op jit(solution)/shard_map/ppermute | solution.py:22
  175.9 17.3 %collective-permute-start.7 = (f32[17,8,1,128]{3,2,1,0:T(1,128)S(1)}, f32[17,8,1,128]{3,2,1,0:T(1,128)S(1)}, u32[]{:S(2)}, u32[]{:S(2)}) collective-permute-start(f32[17,8,1,128]{3,2,1,0:T(1,128)S(1)} %get-tuple-element.18), channel_id=1, source_target_pairs={{8,0},{16,8},{24,16},{32,24},{40,32},{48,40},{56,48},{64,56},{72,6... | collective-permute-start | bytes 208904 | tf_op jit(solution)/shard_map/ppermute | solution.py:24
where the time goes:
time: 196 us
  blocking collectives  101 us (52%)
  starting transfers between devices  79.2 us (40%)
  other arithmetic  8.42 us (4%)
  waiting for transfers between devices  4.03 us (2%)
  local copies, waits for them, and re-layouts  2.72 us (1%)
    psum x2, blocking collectives, square_total(): return lax.psum(jnp.sum(values * values, axis=0), 'param')  101 us
    ppermute x4, starting transfers between devices, with_halo(): lax.ppermute(head, axis, [((i + 1) % count, i) for i in range(ends)])  66.5 us
    ppermute x4, starting transfers between devices, with_halo(): lax.ppermute(tail, axis, [(i, (i + 1) % count) for i in range(ends)])  12.8 us
  transfers between devices with their start and end apart: 8, of which 3 were waited for; matrix products, arithmetic and copies ran while one was open for 0% of the time, Pallas kernels for 0%

commit v1 on v0

v1 whole, which is shorter than its diff:
```python
import functools
import jax
import jax.numpy as jnp
from jax import lax
from jax.experimental import pallas as pl
from jax.experimental.pallas import tpu as pltpu
from jax.sharding import PartitionSpec as P

MESH = pl.DeviceIdType.MESH
DT = 0.05
H0 = 3
OWNERS = (2, 3, 4, 5)


def kernel(nspace, nparam, g_hbm, u_hbm, m_hbm, out, *scratch):
    (G, U, MI, F0, F1, F2, F3, M, HX, HZ, HY, S0, S1, RS0, RS1, T0, T1,
     in_sem, m_s, m_r, h0_s, h0_r, h2_s, h2_r,
     rs0_s, rs0_r, rs1_s, rs1_r, ag0_s, ag0_r, ag1_s, ag1_r, ex0_s, ex0_r, ex1_s, ex1_r) = scratch
    cx, ny, nz = 8, 8, 128
    count = F0.shape[1]
    own = len(OWNERS)
    span = ny // own
    s = lax.axis_index("space")
    p = lax.axis_index("param")
    up = lax.rem(s + 1, nspace)
    down = lax.rem(s + nspace - 1, nspace)

    loads = [
        pltpu.make_async_copy(g_hbm, G, in_sem.at[0]),
        pltpu.make_async_copy(m_hbm, MI, in_sem.at[1]),
        pltpu.make_async_copy(u_hbm, U, in_sem.at[2]),
    ]
    for load in loads:
        load.start()

    barrier = pltpu.get_barrier_semaphore()

    def greet(device):
        pl.semaphore_signal(barrier, inc=1, device_id=device, device_id_type=MESH)

    for k in range(1, nparam):
        greet((s, lax.rem(p + k, nparam)))
    greet((up, p))
    greet((down, p))
    greet((up, OWNERS[0]))
    greet((down, OWNERS[-1]))

    loads[0].wait()
    loads[1].wait()
    for j in range(ny):
        M[j + H0] = MI[pl.ds(j, cx, stride=ny), :]
    loads[2].wait()
    for j in range(ny):
        label = G[pl.ds(j, cx, stride=ny), :] - p * count
        total = None
        for q in range(count):
            value = U[pl.ds(q * cx * ny + j, cx, stride=ny), :]
            value = jnp.where(label == q, 1.0, 0.0) + value
            F0[j + H0, q] = value
            total = value * value if total is None else total + value * value
        S0[j] = total

    is_ender = jnp.logical_or(p == OWNERS[0], p == OWNERS[-1])

    @pl.when(is_ender)
    def _():
        pl.semaphore_wait(barrier, nparam + 1 + nparam)

    @pl.when(jnp.logical_not(is_ender))
    def _():
        pl.semaphore_wait(barrier, nparam + 1)

    def remote(src, dst, send, recv, device):
        return pltpu.make_async_remote_copy(
            src_ref=src, dst_ref=dst, send_sem=send, recv_sem=recv,
            device_id=device, device_id_type=MESH)

    def reduce_copy(S, RS, ss, rr, i, slot):
        return remote(S.at[pl.ds(i * span, span)], RS.at[slot], ss.at[i], rr.at[slot], (s, OWNERS[i]))

    def reduce_start(S, RS, ss, rr):
        for i in range(own):
            @pl.when(p != OWNERS[i])
            def _():
                reduce_copy(S, RS, ss, rr, i, p).start()

    def group_copy(T, edge, ss, rr, i, q):
        rows = T.at[pl.ds(edge + i * span, span)]
        return remote(rows, rows, ss.at[q], rr.at[i], (s, q))

    def edge_copy(T, edge, ss, rr, side, q):
        if side == 0:
            return remote(T.at[pl.ds(ny, edge)], T.at[pl.ds(0, edge)], ss.at[q], rr.at[0], (up, q))
        return remote(T.at[pl.ds(edge, edge)], T.at[pl.ds(edge + ny, edge)], ss.at[q], rr.at[1], (down, q))

    def finish_totals(S, RS, rs_s, rs_r, T, edge, ag_s, ag_r, ex_s, ex_r):
        for i in range(own):
            @pl.when(p == OWNERS[i])
            def _():
                total = S[pl.ds(i * span, span)]
                for q in range(nparam):
                    if q != OWNERS[i]:
                        reduce_copy(S, RS, rs_s, rs_r, i, q).wait_recv()
                        total = total + RS[q]
                T[pl.ds(edge + i * span, span)] = total
                if i == own - 1:
                    for q in range(nparam):
                        edge_copy(T, edge, ex_s, ex_r, 0, q).start()
                if i == 0:
                    for q in reversed(range(nparam)):
                        edge_copy(T, edge, ex_s, ex_r, 1, q).start()
                for d in reversed(range(1, nparam)):
                    for q in (OWNERS[i] - d, OWNERS[i] + d):
                        if 0 <= q < nparam:
                            group_copy(T, edge, ag_s, ag_r, i, q).start()

    def group_wait(T, edge, ag_s, ag_r):
        for i in range(own):
            @pl.when(p != OWNERS[i])
            def _():
                group_copy(T, edge, ag_s, ag_r, i, 0).wait_recv()

    def edge_wait(T, edge, ex_s, ex_r):
        for side in (0, 1):
            edge_copy(T, edge, ex_s, ex_r, side, 0).wait_recv()

    def settle(S, RS, rs_s, rs_r, T, edge, ag_s, ag_r, ex_s, ex_r):
        for i in range(own):
            @pl.when(p != OWNERS[i])
            def _():
                reduce_copy(S, RS, rs_s, rs_r, i, p).wait_send()

            @pl.when(p == OWNERS[i])
            def _():
                for q in range(nparam):
                    if q != OWNERS[i]:
                        group_copy(T, edge, ag_s, ag_r, i, q).wait_send()
                    if i == own - 1:
                        edge_copy(T, edge, ex_s, ex_r, 0, q).wait_send()
                    if i == 0:
                        edge_copy(T, edge, ex_s, ex_r, 1, q).wait_send()

    def halo_pair(F, halo, ss, rr, k):
        return (
            remote(F.at[halo + ny - 1 - k], F.at[halo - 1 - k], ss.at[0, k], rr.at[0, k], (up, p)),
            remote(F.at[halo + k], F.at[halo + ny + k], ss.at[1, k], rr.at[1, k], (down, p)),
        )

    mobility = (
        remote(M.at[pl.ds(ny, H0)], M.at[pl.ds(0, H0)], m_s.at[0], m_r.at[0], (up, p)),
        remote(M.at[pl.ds(H0, H0)], M.at[pl.ds(H0 + ny, H0)], m_s.at[1], m_r.at[1], (down, p)),
    )
    first = [halo_pair(F0, H0, h0_s, h0_r, k) for k in range(H0)]
    second = {k: halo_pair(F2, 2, h2_s, h2_r, k) for k in range(H0 - 2, 2)}

    sum0 = (S0, RS0, rs0_s, rs0_r, T0, H0 - 1, ag0_s, ag0_r, ex0_s, ex0_r)
    sum1 = (S1, RS1, rs1_s, rs1_r, T1, 1, ag1_s, ag1_r, ex1_s, ex1_r)

    reduce_start(S0, RS0, rs0_s, rs0_r)
    for copy in mobility:
        copy.start()
    for pair in first:
        for copy in pair:
            copy.start()

    below = jnp.where(s > 0, 0.5 * DT, 0.0)
    above = jnp.where(s < nspace - 1, 0.5 * DT, 0.0)
    inner_x = jnp.where(lax.broadcasted_iota(jnp.int32, (cx, nz), 0) < cx - 1, 0.5 * DT, 0.0)
    inner_z = jnp.where(lax.broadcasted_iota(jnp.int32, (cx, nz), 1) < nz - 1, 0.5 * DT, 0.0)

    def row_faces(y):
        m = M[y + H0]
        HX[y + H0 - 1] = inner_x * (m + pltpu.roll(m, cx - 1, 0))
        HZ[y + H0 - 1] = inner_z * (m + pltpu.roll(m, nz - 1, 1))

    def column_face(y):
        scale = below if y == -1 else above if y == ny - 1 else 0.5 * DT
        HY[y + H0] = scale * (M[y + H0] + M[y + H0 + 1])

    for y in range(ny):
        row_faces(y)
    for y in range(ny - 1):
        column_face(y)

    def advance(src, so, store, T, edge, lo, hi, S=None):
        def row(y, carry):
            m = M[y + H0]
            linear = 1.0 - (DT * m) * (3.0 * T[y + edge] - 1.0)
            square = (2.0 * DT) * m
            hx = HX[y + H0 - 1]
            hz = HZ[y + H0 - 1]
            hu = HY[y + H0]
            hl = HY[y + H0 - 1]
            total = None
            for q in range(count):
                f = src[y + so, q]
                gx = hx * (pltpu.roll(f, cx - 1, 0) - f)
                gz = hz * (pltpu.roll(f, nz - 1, 1) - f)
                flow = hu * (src[y + so + 1, q] - f) - hl * (f - src[y + so - 1, q])
                flow = flow + ((gx - pltpu.roll(gx, 1, 0)) + (gz - pltpu.roll(gz, 1, 1)))
                value = f * (linear + square * (f * f)) + flow
                store(y, q, value)
                if S is not None:
                    total = value * value if total is None else total + value * value
            if S is not None:
                S[y] = total
            return carry

        if hi - lo == 1:
            row(lo, 0)
        else:
            lax.fori_loop(lo, hi, row, 0)

    def into(F, halo):
        def store(y, q, value):
            F[y + halo, q] = value
        return store

    def emit(y, q, value):
        out[pl.ds(q * cx * ny + y, cx, stride=ny), :] = value

    step1 = functools.partial(advance, F0, H0, into(F1, H0 - 1), T0, H0 - 1)
    step2 = functools.partial(advance, F1, H0 - 1, into(F2, 2), T0, H0 - 1)
    step3 = functools.partial(advance, F2, 2, into(F3, 1), T1, 1)
    step4 = functools.partial(advance, F3, 1, emit, T1, 1)

    finish_totals(*sum0)
    for copy in mobility:
        copy.wait_recv()
    for k in range(H0 - 1):
        row_faces(-1 - k)
        row_faces(ny + k)
    for k in range(H0):
        column_face(-1 - k)
        column_face(ny - 1 + k)

    group_wait(T0, H0 - 1, ag0_s, ag0_r)
    step1(1, ny - 1)
    step2(2, ny - 2, S1)
    for copy in first[0]:
        copy.wait_recv()
    step1(0, 1)
    step1(ny - 1, ny)
    step2(1, 2, S1)
    step2(ny - 2, ny - 1, S1)
    edge_wait(T0, H0 - 1, ex0_s, ex0_r)
    for copy in first[1]:
        copy.wait_recv()
    step1(-1, 0)
    step1(ny, ny + 1)
    step2(0, 1, S1)
    step2(ny - 1, ny, S1)

    reduce_start(S1, RS1, rs1_s, rs1_r)
    for k in second:
        for copy in second[k]:
            copy.start()
    finish_totals(*sum1)
    for k in range(2, H0):
        for copy in first[k]:
            copy.wait_recv()
        step1(-k, 1 - k)
        step1(ny + k - 1, ny + k)
        step2(1 - k, 2 - k)
        step2(ny + k - 2, ny + k - 1)

    group_wait(T1, 1, ag1_s, ag1_r)
    step3(1, ny - 1)
    step4(2, ny - 2)
    if 0 in second:
        for copy in second[0]:
            copy.wait_recv()
    step3(0, 1)
    step3(ny - 1, ny)
    step4(1, 2)
    step4(ny - 2, ny - 1)
    edge_wait(T1, 1, ex1_s, ex1_r)
    if 1 in second:
        for copy in second[1]:
            copy.wait_recv()
    step3(-1, 0)
    step3(ny, ny + 1)
    step4(0, 1)
    step4(ny - 1, ny)

    for copy in mobility:
        copy.wait_send()
    for pair in first + list(second.values()):
        for copy in pair:
            copy.wait_send()
    settle(*sum0)
    settle(*sum1)


def local(nspace, nparam, grain_param, perturbation, mobility):
    count, _, cx, ny, nz = perturbation.shape
    own = len(OWNERS)
    f32 = jnp.float32
    row = (cx, nz)
    hbm = pl.BlockSpec(memory_space=pltpu.HBM)
    dma = pltpu.SemaphoreType.DMA
    sums = [dma((own,)), dma((nparam,))] * 2 + [dma((nparam,)), dma((own,))] * 2 + [dma((nparam,)), dma((2,))] * 2
    out = pl.pallas_call(
        functools.partial(kernel, nspace, nparam),
        out_shape=jax.ShapeDtypeStruct((count * cx * ny, nz), f32),
        in_specs=[hbm] * 3,
        out_specs=pl.BlockSpec(memory_space=pltpu.VMEM),
        scratch_shapes=[
            pltpu.VMEM((cx * ny, nz), jnp.int32),
            pltpu.VMEM((count * cx * ny, nz), f32),
            pltpu.VMEM((cx * ny, nz), f32),
            pltpu.VMEM((ny + 2 * H0, count) + row, f32),
            pltpu.VMEM((ny + 2 * H0 - 2, count) + row, f32),
            pltpu.VMEM((ny + 4, count) + row, f32),
            pltpu.VMEM((ny + 2, count) + row, f32),
            pltpu.VMEM((ny + 2 * H0,) + row, f32),
            pltpu.VMEM((ny + 2 * H0 - 2,) + row, f32),
            pltpu.VMEM((ny + 2 * H0 - 2,) + row, f32),
            pltpu.VMEM((ny + 2 * H0 - 1,) + row, f32),
            pltpu.VMEM((ny,) + row, f32),
            pltpu.VMEM((ny,) + row, f32),
            pltpu.VMEM((nparam, ny // own) + row, f32),
            pltpu.VMEM((nparam, ny // own) + row, f32),
            pltpu.VMEM((ny + 2 * H0 - 2,) + row, f32),
            pltpu.VMEM((ny + 2,) + row, f32),
            dma((3,)),
            dma((2,)), dma((2,)),
            dma((2, H0)), dma((2, H0)),
            dma((2, 2)), dma((2, 2)),
        ] + sums,
        compiler_params=pltpu.CompilerParams(
            collective_id=0, has_side_effects=True, vmem_limit_bytes=32 << 20),
        cost_estimate=pl.CostEstimate(flops=12_000_000, bytes_accessed=1_200_000, transcendentals=0),
    )(
        grain_param.reshape(cx * ny, nz),
        perturbation.reshape(count * cx * ny, nz),
        mobility.reshape(cx * ny, nz),
    )
    return out.reshape(perturbation.shape)


def solution(mesh):
    nspace, nparam = mesh.shape["space"], mesh.shape["param"]
    in_specs = (
        P("space", None, None, None),
        P("param", "space", None, None, None),
        P("space", None, None, None),
    )
    out_specs = P("param", "space", None, None, None)
    return jax.shard_map(
        functools.partial(local, nspace, nparam), mesh=mesh, in_specs=in_specs, out_specs=out_specs, check_vma=False)
```

time: 196 us -> 71.3 us (0.36)
  the two profiles are of different devices: /device:TPU:6 before, /device:TPU:32 now
where the time goes in v1:
time: 71.3 us; the launch traced here: 71 us
  Pallas kernels  67.6 us (95%)
  local copies, waits for them, and re-layouts  3.35 us (5%)
    pallas_call x1, Pallas kernels, local(): pl.pallas_call(functools.partial(kernel, nspace, nparam), out_shape=jax.S...  67.6 us
    unnamed x7, local copies, waits for them, and re-layouts  3.35 us

profile of v1, /device:TPU:32, one launch (start us, length us, event | category | flops | bytes accessed | tf_op | source)
XLA Modules:
  0.0 71.0 jit_solution(14150328513776830347)
XLA Ops:
  0.0 0.0 copy-start
  0.0 1.0 %copy-done = f32[16,1,8,8,128]{4,3,2,1,0:T(8,128)S(1)} copy-done((f32[16,1,8,8,128]{4,3,2,1,0:T(8,128)S(1)}, f32[16,1,8,8,128]{4,3,2,1,0:T(8,128)}, u32[]{:S(2)}) %copy-start) | copy-done | bytes 524312
  1.0 0.0 copy-start.1
  1.0 0.8 %copy-done.1 = s32[1,8,8,128]{3,2,1,0:T(8,128)S(1)} copy-done((s32[1,8,8,128]{3,2,1,0:T(8,128)S(1)}, s32[1,8,8,128]{3,2,1,0:T(8,128)}, u32[]{:S(2)}) %copy-start.1) | copy-done | bytes 32792
  1.8 0.0 copy-start.2
  1.8 0.8 %copy-done.2 = f32[1,8,8,128]{3,2,1,0:T(8,128)S(1)} copy-done((f32[1,8,8,128]{3,2,1,0:T(8,128)S(1)}, f32[1,8,8,128]{3,2,1,0:T(8,128)}, u32[]{:S(2)}) %copy-start.2) | copy-done | bytes 32792
  2.6 67.6 %shard_map.37 = f32[1024,128]{1,0:T(8,128)S(1)} custom-call(s32[64,128]{1,0:T(8,128)S(1)} %bitcast.8, f32[1024,128]{1,0:T(8,128)S(1)} %bitcast.7, f32[64,128]{1,0:T(8,128)S(1)} %bitcast.9), custom_call_target="tpu_custom_call" | custom-call | flops 12000000 | bytes 1200000 | tf_op jit(solution)/shard_map/pallas_call | solution.py:303
  70.2 0.8 %copy.6 = f32[16,1,8,8,128]{4,3,2,1,0:T(8,128)} copy(f32[16,1,8,8,128]{4,3,2,1,0:T(8,128)S(1)} %bitcast.6) | data formatting | bytes 1048576
Async XLA Ops:
  0.0 1.0 %copy-start = (f32[16,1,8,8,128]{4,3,2,1,0:T(8,128)S(1)}, f32[16,1,8,8,128]{4,3,2,1,0:T(8,128)}, u32[]{:S(2)}) copy-start(f32[16,1,8,8,128]{4,3,2,1,0:T(8,128)} %param.4) | copy-start | bytes 1572868
  1.0 0.8 %copy-start.1 = (s32[1,8,8,128]{3,2,1,0:T(8,128)S(1)}, s32[1,8,8,128]{3,2,1,0:T(8,128)}, u32[]{:S(2)}) copy-start(s32[1,8,8,128]{3,2,1,0:T(8,128)} %param.3) | copy-start | bytes 98308
  1.8 0.8 %copy-start.2 = (f32[1,8,8,128]{3,2,1,0:T(8,128)S(1)}, f32[1,8,8,128]{3,2,1,0:T(8,128)}, u32[]{:S(2)}) copy-start(f32[1,8,8,128]{3,2,1,0:T(8,128)} %param.5) | copy-start | bytes 98308

commit v2 on v1

--- a/solution.py
+++ b/solution.py
@@ -8,7 +8,7 @@
 
 MESH = pl.DeviceIdType.MESH
 DT = 0.05
-H0 = 3
+H0 = 2
 OWNERS = (2, 3, 4, 5)
 
 
@@ -24,6 +24,9 @@
     p = lax.axis_index("param")
     up = lax.rem(s + 1, nspace)
     down = lax.rem(s + nspace - 1, nspace)
+    sides = (s < nspace - 1, s > 0)
+    up_count = jnp.where(sides[0], 1, 0)
+    down_count = jnp.where(sides[1], 1, 0)
 
     loads = [
         pltpu.make_async_copy(g_hbm, G, in_sem.at[0]),
@@ -40,10 +43,16 @@
 
     for k in range(1, nparam):
         greet((s, lax.rem(p + k, nparam)))
-    greet((up, p))
-    greet((down, p))
-    greet((up, OWNERS[0]))
-    greet((down, OWNERS[-1]))
+
+    @pl.when(sides[0])
+    def _():
+        greet((up, p))
+        greet((up, OWNERS[0]))
+
+    @pl.when(sides[1])
+    def _():
+        greet((down, p))
+        greet((down, OWNERS[-1]))
 
     loads[0].wait()
     loads[1].wait()
@@ -60,26 +69,55 @@
             total = value * value if total is None else total + value * value
         S0[j] = total
 
-    is_ender = jnp.logical_or(p == OWNERS[0], p == OWNERS[-1])
-
-    @pl.when(is_ender)
+    def blank(low, refs):
+        for ref, halo in refs:
+            for k in range(halo):
+                row = ref.at[halo - 1 - k] if low else ref.at[halo + ny + k]
+                row[...] = jnp.zeros_like(row)
+
+    beyond = ((F0, H0), (F2, 2), (M, H0), (T0, H0 - 1), (T1, 1))
+
+    @pl.when(jnp.logical_not(sides[1]))
     def _():
-        pl.semaphore_wait(barrier, nparam + 1 + nparam)
-
-    @pl.when(jnp.logical_not(is_ender))
+        blank(True, beyond)
+
+    @pl.when(jnp.logical_not(sides[0]))
     def _():
-        pl.semaphore_wait(barrier, nparam + 1)
+        blank(False, beyond)
+
+    heard = nparam - 1 + up_count + down_count
+    heard = heard + jnp.where(p == OWNERS[0], nparam, 0) * down_count
+    heard = heard + jnp.where(p == OWNERS[-1], nparam, 0) * up_count
+    pl.semaphore_wait(barrier, heard)
 
     def remote(src, dst, send, recv, device):
         return pltpu.make_async_remote_copy(
             src_ref=src, dst_ref=dst, send_sem=send, recv_sem=recv,
             device_id=device, device_id_type=MESH)
 
+    def start_sided(copies):
+        for side in (0, 1):
+            @pl.when(sides[side])
+            def _():
+                copies[side].start()
+
+    def sent_sided(copies):
+        for side in (0, 1):
+            @pl.when(sides[side])
+            def _():
+                copies[side].wait_send()
+
+    def arrived_sided(copies):
+        for side in (0, 1):
+            @pl.when(sides[1 - side])
+            def _():
+                copies[side].wait_recv()
+
     def reduce_copy(S, RS, ss, rr, i, slot):
         return remote(S.at[pl.ds(i * span, span)], RS.at[slot], ss.at[i], rr.at[slot], (s, OWNERS[i]))
 
-    def reduce_start(S, RS, ss, rr):
-        for i in range(own):
+    def reduce_start(S, RS, ss, rr, which=range(own)):
+        for i in which:
             @pl.when(p != OWNERS[i])
             def _():
                 reduce_copy(S, RS, ss, rr, i, p).start()
@@ -104,11 +142,15 @@
                         total = total + RS[q]
                 T[pl.ds(edge + i * span, span)] = total
                 if i == own - 1:
-                    for q in range(nparam):
-                        edge_copy(T, edge, ex_s, ex_r, 0, q).start()
+                    @pl.when(sides[0])
+                    def _():
+                        for q in range(nparam):
+                            edge_copy(T, edge, ex_s, ex_r, 0, q).start()
                 if i == 0:
-                    for q in reversed(range(nparam)):
-                        edge_copy(T, edge, ex_s, ex_r, 1, q).start()
+                    @pl.when(sides[1])
+                    def _():
+                        for q in reversed(range(nparam)):
+                            edge_copy(T, edge, ex_s, ex_r, 1, q).start()
                 for d in reversed(range(1, nparam)):
                     for q in (OWNERS[i] - d, OWNERS[i] + d):
                         if 0 <= q < nparam:
@@ -121,8 +163,7 @@
                 group_copy(T, edge, ag_s, ag_r, i, 0).wait_recv()
 
     def edge_wait(T, edge, ex_s, ex_r):
-        for side in (0, 1):
-            edge_copy(T, edge, ex_s, ex_r, side, 0).wait_recv()
+        arrived_sided([edge_copy(T, edge, ex_s, ex_r, side, 0) for side in (0, 1)])
 
     def settle(S, RS, rs_s, rs_r, T, edge, ag_s, ag_r, ex_s, ex_r):
         for i in range(own):
@@ -135,10 +176,12 @@
                 for q in range(nparam):
                     if q != OWNERS[i]:
                         group_copy(T, edge, ag_s, ag_r, i, q).wait_send()
-                    if i == own - 1:
-                        edge_copy(T, edge, ex_s, ex_r, 0, q).wait_send()
-                    if i == 0:
-                        edge_copy(T, edge, ex_s, ex_r, 1, q).wait_send()
+                for side, j in ((0, own - 1), (1, 0)):
+                    if i == j:
+                        @pl.when(sides[side])
+                        def _():
+                            for q in range(nparam):
+                                edge_copy(T, edge, ex_s, ex_r, side, q).wait_send()
 
     def halo_pair(F, halo, ss, rr, k):
         return (
@@ -157,11 +200,10 @@
     sum1 = (S1, RS1, rs1_s, rs1_r, T1, 1, ag1_s, ag1_r, ex1_s, ex1_r)
 
     reduce_start(S0, RS0, rs0_s, rs0_r)
-    for copy in mobility:
-        copy.start()
-    for pair in first:
-        for copy in pair:
-            copy.start()
+    start_sided(mobility)
+    start_sided(first[0])
+
+    start_sided(first[1])
 
     below = jnp.where(s > 0, 0.5 * DT, 0.0)
     above = jnp.where(s < nspace - 1, 0.5 * DT, 0.0)
@@ -225,8 +267,8 @@
     step4 = functools.partial(advance, F3, 1, emit, T1, 1)
 
     finish_totals(*sum0)
-    for copy in mobility:
-        copy.wait_recv()
+
+    arrived_sided(mobility)
     for k in range(H0 - 1):
         row_faces(-1 - k)
         row_faces(ny + k)
@@ -237,28 +279,27 @@
     group_wait(T0, H0 - 1, ag0_s, ag0_r)
     step1(1, ny - 1)
     step2(2, ny - 2, S1)
-    for copy in first[0]:
-        copy.wait_recv()
+    reduce_start(S1, RS1, rs1_s, rs1_r, (1, 2))
+    arrived_sided(first[0])
     step1(0, 1)
     step1(ny - 1, ny)
     step2(1, 2, S1)
     step2(ny - 2, ny - 1, S1)
+    start_sided(second[1])
     edge_wait(T0, H0 - 1, ex0_s, ex0_r)
-    for copy in first[1]:
-        copy.wait_recv()
+    arrived_sided(first[1])
     step1(-1, 0)
     step1(ny, ny + 1)
     step2(0, 1, S1)
     step2(ny - 1, ny, S1)
 
-    reduce_start(S1, RS1, rs1_s, rs1_r)
-    for k in second:
-        for copy in second[k]:
-            copy.start()
+    reduce_start(S1, RS1, rs1_s, rs1_r, (0, 3))
+
+    start_sided(second[0])
     finish_totals(*sum1)
+
     for k in range(2, H0):
-        for copy in first[k]:
-            copy.wait_recv()
+        arrived_sided(first[k])
         step1(-k, 1 - k)
         step1(ny + k - 1, ny + k)
         step2(1 - k, 2 - k)
@@ -268,26 +309,21 @@
     step3(1, ny - 1)
     step4(2, ny - 2)
     if 0 in second:
-        for copy in second[0]:
-            copy.wait_recv()
+        arrived_sided(second[0])
     step3(0, 1)
     step3(ny - 1, ny)
     step4(1, 2)
     step4(ny - 2, ny - 1)
     edge_wait(T1, 1, ex1_s, ex1_r)
     if 1 in second:
-        for copy in second[1]:
-            copy.wait_recv()
+        arrived_sided(second[1])
     step3(-1, 0)
     step3(ny, ny + 1)
     step4(0, 1)
     step4(ny - 1, ny)
 
-    for copy in mobility:
-        copy.wait_send()
-    for pair in first + list(second.values()):
-        for copy in pair:
-            copy.wait_send()
+    for pair in [mobility] + first + list(second.values()):
+        sent_sided(pair)
     settle(*sum0)
     settle(*sum1)
 
@@ -329,7 +365,7 @@
             dma((2, 2)), dma((2, 2)),
         ] + sums,
         compiler_params=pltpu.CompilerParams(
-            collective_id=0, has_side_effects=True, vmem_limit_bytes=32 << 20),
+            collective_id=0, has_side_effects=True, vmem_limit_bytes=60 << 20),
         cost_estimate=pl.CostEstimate(flops=12_000_000, bytes_accessed=1_200_000, transcendentals=0),
     )(
         grain_param.reshape(cx * ny, nz),

time: 71.3 us -> 66.6 us (0.934)
  the two profiles are of different devices: /device:TPU:32 before, /device:TPU:28 now
where the time goes in v2:
time: 66.6 us; the launch traced here: 66.4 us
  Pallas kernels  64.5 us (97%)
  local copies, waits for them, and re-layouts  1.89 us (3%)
    pallas_call x1, Pallas kernels, local(): pl.pallas_call(functools.partial(kernel, nspace, nparam), out_shape=jax.S...  64.5 us
    unnamed x1, local copies, waits for them, and re-layouts  1.89 us

profile of v2, /device:TPU:28, one launch (start us, length us, event | category | flops | bytes accessed | tf_op | source)
XLA Modules:
  0.0 66.4 jit_solution(6449454975692059222)
XLA Ops:
  0.0 64.5 %shard_map.37 = f32[1024,128]{1,0:T(8,128)} custom-call(s32[64,128]{1,0:T(8,128)} %bitcast.8, f32[1024,128]{1,0:T(8,128)} %bitcast.7, f32[64,128]{1,0:T(8,128)} %bitcast.9), custom_call_target="tpu_custom_call" | custom-call | flops 12000000 | bytes 1200000 | tf_op jit(solution)/shard_map/pallas_call | solution.py:339
  64.5 1.9 %copy.6 = f32[16,1,8,8,128]{4,3,2,1,0:T(8,128)} copy(f32[16,1,8,8,128]{4,3,2,1,0:T(8,128)} %bitcast.6) | data formatting | bytes 1048576

commit v3 on v2

--- a/solution.py
+++ b/solution.py
@@ -10,10 +10,11 @@
 DT = 0.05
 H0 = 2
 OWNERS = (2, 3, 4, 5)
-
-
-def kernel(nspace, nparam, g_hbm, u_hbm, m_hbm, out, *scratch):
-    (G, U, MI, F0, F1, F2, F3, M, HX, HZ, HY, S0, S1, RS0, RS1, T0, T1,
+OUT_PARTS = 4
+
+
+def kernel(nspace, nparam, g_hbm, u_hbm, m_hbm, out_hbm, *scratch):
+    (out, out_sem, G, U, MI, F0, F1, F2, F3, M, HX, HZ, HY, S0, S1, RS0, RS1, T0, T1,
      in_sem, m_s, m_r, h0_s, h0_r, h2_s, h2_r,
      rs0_s, rs0_r, rs1_s, rs1_r, ag0_s, ag0_r, ag1_s, ag1_r, ex0_s, ex0_r, ex1_s, ex1_r) = scratch
     cx, ny, nz = 8, 8, 128
@@ -224,7 +225,7 @@
     for y in range(ny - 1):
         column_face(y)
 
-    def advance(src, so, store, T, edge, lo, hi, S=None):
+    def advance(src, so, store, T, edge, lo, hi, S=None, fields=None):
         def row(y, carry):
             m = M[y + H0]
             linear = 1.0 - (DT * m) * (3.0 * T[y + edge] - 1.0)
@@ -234,7 +235,7 @@
             hu = HY[y + H0]
             hl = HY[y + H0 - 1]
             total = None
-            for q in range(count):
+            for q in fields or range(count):
                 f = src[y + so, q]
                 gx = hx * (pltpu.roll(f, cx - 1, 0) - f)
                 gz = hz * (pltpu.roll(f, nz - 1, 1) - f)
@@ -295,8 +296,18 @@
 
     reduce_start(S1, RS1, rs1_s, rs1_r, (0, 3))
 
-    start_sided(second[0])
+    is_owner = functools.reduce(jnp.logical_or, [p == o for o in OWNERS])
+
+    @pl.when(jnp.logical_not(is_owner))
+    def _():
+        start_sided(second[0])
+
     finish_totals(*sum1)
+
+    @pl.when(is_owner)
+    def _():
+        start_sided(second[0])
+
 
     for k in range(2, H0):
         arrived_sided(first[k])
@@ -317,15 +328,25 @@
     edge_wait(T1, 1, ex1_s, ex1_r)
     if 1 in second:
         arrived_sided(second[1])
-    step3(-1, 0)
-    step3(ny, ny + 1)
-    step4(0, 1)
-    step4(ny - 1, ny)
+    part = count // OUT_PARTS
+    writes = []
+    for c in range(OUT_PARTS):
+        fields = range(c * part, (c + 1) * part)
+        step3(-1, 0, fields=fields)
+        step3(ny, ny + 1, fields=fields)
+        step4(0, 1, fields=fields)
+        step4(ny - 1, ny, fields=fields)
+        run = pl.ds(c * part * cx * ny, part * cx * ny)
+        write = pltpu.make_async_copy(out.at[run], out_hbm.at[run], out_sem.at[c])
+        write.start()
+        writes.append(write)
 
     for pair in [mobility] + first + list(second.values()):
         sent_sided(pair)
     settle(*sum0)
     settle(*sum1)
+    for write in writes:
+        write.wait()
 
 
 def local(nspace, nparam, grain_param, perturbation, mobility):
@@ -340,8 +361,10 @@
         functools.partial(kernel, nspace, nparam),
         out_shape=jax.ShapeDtypeStruct((count * cx * ny, nz), f32),
         in_specs=[hbm] * 3,
-        out_specs=pl.BlockSpec(memory_space=pltpu.VMEM),
+        out_specs=hbm,
         scratch_shapes=[
+            pltpu.VMEM((count * cx * ny, nz), f32),
+            dma((OUT_PARTS,)),
             pltpu.VMEM((cx * ny, nz), jnp.int32),
             pltpu.VMEM((count * cx * ny, nz), f32),
             pltpu.VMEM((cx * ny, nz), f32),

time: 66.6 us -> 65.4 us (0.982)
  the two profiles are of different devices: /device:TPU:28 before, /device:TPU:65 now
where the time goes in v3:
time: 65.4 us; the launch traced here: 65.2 us
  Pallas kernels  63.3 us (97%)
  local copies, waits for them, and re-layouts  1.89 us (3%)
    pallas_call x1, Pallas kernels, local(): pl.pallas_call(functools.partial(kernel, nspace, nparam), out_shape=jax.S...  63.3 us
    unnamed x1, local copies, waits for them, and re-layouts  1.89 us

profile of v3, /device:TPU:65, one launch (start us, length us, event | category | flops | bytes accessed | tf_op | source)
XLA Modules:
  0.0 65.2 jit_solution(8448626790070897730)
XLA Ops:
  0.0 63.3 %shard_map.37 = f32[1024,128]{1,0:T(8,128)} custom-call(s32[64,128]{1,0:T(8,128)} %bitcast.8, f32[1024,128]{1,0:T(8,128)} %bitcast.7, f32[64,128]{1,0:T(8,128)} %bitcast.9), custom_call_target="tpu_custom_call" | custom-call | flops 12000000 | bytes 1200000 | tf_op jit(solution)/shard_map/pallas_call | solution.py:360
  63.3 1.9 %copy.6 = f32[16,1,8,8,128]{4,3,2,1,0:T(8,128)} copy(f32[16,1,8,8,128]{4,3,2,1,0:T(8,128)} %bitcast.6) | data formatting | bytes 1048576

commit v4 on v3

--- a/solution.py
+++ b/solution.py
@@ -260,7 +260,7 @@
         return store
 
     def emit(y, q, value):
-        out[pl.ds(q * cx * ny + y, cx, stride=ny), :] = value
+        out[pl.ds(q * cx * ny + y, cx, stride=ny), :] = 0.5 * value
 
     step1 = functools.partial(advance, F0, H0, into(F1, H0 - 1), T0, H0 - 1)
     step2 = functools.partial(advance, F1, H0 - 1, into(F2, 2), T0, H0 - 1)
@@ -395,7 +395,7 @@
         perturbation.reshape(count * cx * ny, nz),
         mobility.reshape(cx * ny, nz),
     )
-    return out.reshape(perturbation.shape)
+    return 2.0 * out.reshape(perturbation.shape)
 
 
 def solution(mesh):

time: 65.4 us -> 65.4 us (level)
  local copies, waits for them, and re-layouts: 1.89 us -> 0 us
  other arithmetic: 0 us -> 1.87 us
    unnamed x1 -> x0, local copies, waits for them, and re-layouts: 1.89 us -> none
    mul x0 -> x1, other arithmetic: none -> 1.87 us  [local(): return 2.0 * out.reshape(perturbation.shape)]
where the time goes in v4:
time: 65.4 us; the launch traced here: 65.2 us
  Pallas kernels  63.3 us (97%)
  other arithmetic  1.87 us (3%)
    pallas_call x1, Pallas kernels, local(): pl.pallas_call(functools.partial(kernel, nspace, nparam), out_shape=jax.S...  63.3 us
    mul x1, other arithmetic, local(): return 2.0 * out.reshape(perturbation.shape)  1.87 us

profile of v4, /device:TPU:65, one launch (start us, length us, event | category | flops | bytes accessed | tf_op | source)
XLA Modules:
  0.0 65.2 jit_solution(8638159834742986382)
XLA Ops:
  0.0 63.3 %shard_map.37 = f32[1024,128]{1,0:T(8,128)} custom-call(s32[64,128]{1,0:T(8,128)} %bitcast.7, f32[1024,128]{1,0:T(8,128)} %bitcast.6, f32[64,128]{1,0:T(8,128)} %bitcast.8), custom_call_target="tpu_custom_call" | custom-call | flops 12000000 | bytes 1200000 | tf_op jit(solution)/shard_map/pallas_call | solution.py:360
  63.3 1.9 %broadcast_multiply_fusion = f32[1024,128]{1,0:T(8,128)} fusion(f32[1024,128]{1,0:T(8,128)} %shard_map.37), kind=kLoop, calls=%fused_computation | loop fusion | flops 131072 | bytes 1048576 | tf_op jit(solution)/shard_map/mul | solution.py:398

commit v5 on v3

--- a/solution.py
+++ b/solution.py
@@ -195,7 +195,18 @@
         remote(M.at[pl.ds(H0, H0)], M.at[pl.ds(H0 + ny, H0)], m_s.at[1], m_r.at[1], (down, p)),
     )
     first = [halo_pair(F0, H0, h0_s, h0_r, k) for k in range(H0)]
-    second = {k: halo_pair(F2, 2, h2_s, h2_r, k) for k in range(H0 - 2, 2)}
+    second = {1: halo_pair(F2, 2, h2_s, h2_r, 1)}
+
+    def near_half(c):
+        half = count // 2
+        part = F2.at[:, pl.ds(c * half, half)]
+        slot = 2 * c
+        return (
+            remote(part.at[1 + ny], part.at[1], h2_s.at[0, slot], h2_r.at[0, slot], (up, p)),
+            remote(part.at[2], part.at[2 + ny], h2_s.at[1, slot], h2_r.at[1, slot], (down, p)),
+        )
+
+    near = [near_half(c) for c in (0, 1)]
 
     sum0 = (S0, RS0, rs0_s, rs0_r, T0, H0 - 1, ag0_s, ag0_r, ex0_s, ex0_r)
     sum1 = (S1, RS1, rs1_s, rs1_r, T1, 1, ag1_s, ag1_r, ex1_s, ex1_r)
@@ -296,18 +307,27 @@
 
     reduce_start(S1, RS1, rs1_s, rs1_r, (0, 3))
 
-    is_owner = functools.reduce(jnp.logical_or, [p == o for o in OWNERS])
+    is_inner = functools.reduce(jnp.logical_or, [p == o for o in OWNERS[1:-1]])
+    is_outer = jnp.logical_or(p == OWNERS[0], p == OWNERS[-1])
+    is_owner = jnp.logical_or(is_inner, is_outer)
+
+    @pl.when(jnp.logical_not(is_inner))
+    def _():
+        start_sided(near[0])
 
     @pl.when(jnp.logical_not(is_owner))
     def _():
-        start_sided(second[0])
+        start_sided(near[1])
 
     finish_totals(*sum1)
 
+    @pl.when(is_inner)
+    def _():
+        start_sided(near[0])
+
     @pl.when(is_owner)
     def _():
-        start_sided(second[0])
-
+        start_sided(near[1])
 
     for k in range(2, H0):
         arrived_sided(first[k])
@@ -319,15 +339,14 @@
     group_wait(T1, 1, ag1_s, ag1_r)
     step3(1, ny - 1)
     step4(2, ny - 2)
-    if 0 in second:
-        arrived_sided(second[0])
+    for pair in near:
+        arrived_sided(pair)
     step3(0, 1)
     step3(ny - 1, ny)
     step4(1, 2)
     step4(ny - 2, ny - 1)
     edge_wait(T1, 1, ex1_s, ex1_r)
-    if 1 in second:
-        arrived_sided(second[1])
+    arrived_sided(second[1])
     part = count // OUT_PARTS
     writes = []
     for c in range(OUT_PARTS):
@@ -341,7 +360,7 @@
         write.start()
         writes.append(write)
 
-    for pair in [mobility] + first + list(second.values()):
+    for pair in [mobility] + first + near + [second[1]]:
         sent_sided(pair)
     settle(*sum0)
     settle(*sum1)
@@ -385,7 +404,7 @@
             dma((3,)),
             dma((2,)), dma((2,)),
             dma((2, H0)), dma((2, H0)),
-            dma((2, 2)), dma((2, 2)),
+            dma((2, 3)), dma((2, 3)),
         ] + sums,
         compiler_params=pltpu.CompilerParams(
             collective_id=0, has_side_effects=True, vmem_limit_bytes=60 << 20),

time: 65.4 us -> 65.8 us (level)
  the two profiles are of different devices: /device:TPU:65 before, /device:TPU:28 now
where the time goes in v5:
time: 65.8 us; the launch traced here: 65.6 us
  Pallas kernels  63.7 us (97%)
  local copies, waits for them, and re-layouts  1.89 us (3%)
    pallas_call x1, Pallas kernels, local(): pl.pallas_call(functools.partial(kernel, nspace, nparam), out_shape=jax.S...  63.7 us
    unnamed x1, local copies, waits for them, and re-layouts  1.89 us

profile of v5, /device:TPU:28, one launch (start us, length us, event | category | flops | bytes accessed | tf_op | source)
XLA Modules:
  0.0 65.6 jit_solution(12286106122278420397)
XLA Ops:
  0.0 63.7 %shard_map.37 = f32[1024,128]{1,0:T(8,128)} custom-call(s32[64,128]{1,0:T(8,128)} %bitcast.8, f32[1024,128]{1,0:T(8,128)} %bitcast.7, f32[64,128]{1,0:T(8,128)} %bitcast.9), custom_call_target="tpu_custom_call" | custom-call | flops 12000000 | bytes 1200000 | tf_op jit(solution)/shard_map/pallas_call | solution.py:379
  63.7 1.9 %copy.6 = f32[16,1,8,8,128]{4,3,2,1,0:T(8,128)} copy(f32[16,1,8,8,128]{4,3,2,1,0:T(8,128)} %bitcast.6) | data formatting | bytes 1048576
